TPU v7x, 768 devices: a whole 4x8x12 slice. The times are simulated.
768 devices in a mesh: row: 24 (over x, z_lo, core), col: 32 (over z_hi, y).
Axes of the slice: x: 4, y: 8, z: 12 (z_hi: 4, z_lo: 3; z = z_hi * 3 + z_lo), core: 2. Of those that a mesh axis runs over, the one named last changes fastest.
Arguments:
- vectors: bfloat16 [1, 16, 24576], P(None, None, ('col', 'row')), may hold values from -110 to 110
- h_tiles: bfloat16 [1, 24, 1024, 128, 128], P(None, 'row', 'col'), may hold values from -0.0625 to 0.0625
- h_list: int32 [1, 24, 1024], P(None, 'row', 'col'), may hold values from -1 to 47, as said below
- j_tiles: bfloat16 [1, 24, 384, 128, 128], P(None, 'row', 'col'), may hold values from -0.109375 to 0.109375
- j_list: int32 [1, 24, 384], P(None, 'row', 'col'), may hold values from -1 to 95, as said below
Outputs:
- basis: float32 [1, 16, 24576], P(None, None, ('row', 'col'))
- transitions: float32 [1, 2, 16, 16], replicated
Inputs may be any that keep to these rules, and one draw needn't show every extreme that they name: `h_list`: each block's 32 entries list distinct tile positions first and then -1; at most 32 positions a block, and some block lists all 32. `j_list`: each block's 12 entries list distinct codes first and then -1; at most 12 codes a block, and some block lists all 12.
All inputs are finite; a program needn't handle non-finite values.
Results may differ from a plain program's by a relative error of at most 0.0003.
Values may be sent and summed in bfloat16 or wider, within the bound.
A program may use at most 64 MiB of HBM per device.

v0:
```python
import jax
import jax.numpy as jnp
from jax import lax
from jax.sharding import Mesh
from jax.sharding import PartitionSpec as P

NSIT = 6
COL = ("col_0", "col_1")
ROW = ("row_0", "row_1", "row_2")
ROW_COL = ("row_0", "row_1", "row_2", "col_0", "col_1")
COL_ROW = ("col_0", "col_1", "row_0", "row_1", "row_2")


exact_precision = lax.Precision.HIGHEST


def joined_along(pieces, dim):
    shape = list(pieces.shape[1:])
    shape[dim] *= pieces.shape[0]
    return jnp.moveaxis(pieces, 0, dim).reshape(shape)


def sent_to_all(value, axis):
    peers = lax.axis_size(axis)
    return lax.all_to_all(
        jnp.broadcast_to(value[None], (peers, *value.shape)), axis, 0, 0, tiled=True
    )


def gather_directly(value, axis, dim):
    return joined_along(sent_to_all(value, axis), dim)


def split_up(value, dim, peers):
    shape = value.shape
    pieces = value.reshape(*shape[:dim], peers, shape[dim] // peers, *shape[dim + 1 :])
    return jnp.moveaxis(pieces, dim, 0)


def sent_and_summed(value, axis, dim):
    peers = lax.axis_size(axis)
    pieces = lax.all_to_all(split_up(value, dim, peers), axis, 0, 0, tiled=True)
    return jnp.sum(pieces, axis=0)


def side_by_side(arrays, axis, dim, along):
    both = jnp.concatenate(arrays, axis=along)
    filled, at, done = (sent_and_summed(both, axis, dim), 0, [])
    for a in arrays:
        done.append(lax.slice_in_dim(filled, at, at + a.shape[along], axis=along))
        at += a.shape[along]
    return tuple(done)


def over_axes(value, axes):
    for axis in axes:
        value = lax.psum(value, axis)
    return value


def local_product(tile_data, code_data, vector_block, operator_count, row_tiles):
    sector_count = tile_data.shape[0]
    tile_size = tile_data.shape[2]
    vector_count = vector_block.shape[1]
    column_tiles = vector_block.shape[2] // tile_size
    position_count = row_tiles * column_tiles
    column_vectors = vector_block.reshape(sector_count, vector_count, column_tiles, tile_size)
    places = code_data % position_count
    operator = code_data // position_count
    column_hot = (
        places[:, :, None] % column_tiles == jnp.arange(column_tiles)[None, None, :]
    ).astype(jnp.bfloat16)
    picked = jnp.einsum(
        "sqc,skcb->sqkb", column_hot, column_vectors, preferred_element_type=jnp.float32
    ).astype(jnp.bfloat16)
    product = jnp.einsum("sqab,sqkb->sqka", tile_data, picked, preferred_element_type=jnp.float32)
    row_hot = (
        (operator[:, :, None, None] == jnp.arange(operator_count)[None, None, :, None])
        & (places[:, :, None, None] // column_tiles == jnp.arange(row_tiles)[None, None, None, :])
        & (code_data[:, :, None, None] >= 0)
    ).astype(jnp.float32)
    result = jnp.einsum("sqor,sqka->sokra", row_hot, product, precision=exact_precision)
    return result.reshape(sector_count, operator_count * vector_count, row_tiles * tile_size)


def inverse_root_of(gram, vector_count):
    scale = jnp.sqrt(jnp.sum(gram * gram, axis=(1, 2), keepdims=True) + 1e-06)
    iterate = gram / scale
    identity = jnp.eye(vector_count, dtype=jnp.float32)[None]
    inverse_root = identity
    for iteration in range(NSIT):
        middle = 1.5 * identity - 0.5 * jnp.einsum(
            "skm,sml->skl", inverse_root, iterate, precision=exact_precision
        )
        iterate = jnp.einsum("skm,sml->skl", iterate, middle, precision=exact_precision)
        inverse_root = jnp.einsum("skm,sml->skl", middle, inverse_root, precision=exact_precision)
    return (inverse_root, scale)


def per_device(vectors, h_tiles, h_list, j_tiles, j_list):
    sector_count = vectors.shape[0]
    vector_count = vectors.shape[1]
    tile_size = h_tiles.shape[-1]
    block_rows = vectors.shape[2] * lax.axis_size(COL)
    total_rows = block_rows * lax.axis_size(ROW)
    row_tiles = block_rows // tile_size
    vector_block = gather_directly(vectors, ROW, 2)
    h_part = local_product(
        h_tiles.reshape(sector_count, -1, tile_size, tile_size),
        h_list.reshape(sector_count, -1),
        vector_block,
        1,
        row_tiles,
    )
    j_part = local_product(
        j_tiles.reshape(sector_count, -1, tile_size, tile_size),
        j_list.reshape(sector_count, -1),
        vector_block,
        2,
        row_tiles,
    )
    projected, applied = side_by_side((h_part, j_part), COL, 2, 1)
    gram_part = jnp.einsum("skp,slp->skl", projected, projected, precision=exact_precision)
    cross_part = jnp.einsum("skp,smp->skm", projected, applied, precision=exact_precision)
    gram, cross = (over_axes(gram_part, ROW_COL), over_axes(cross_part, ROW_COL))
    inverse_root, scale = inverse_root_of(gram, vector_count)
    basis = jnp.sqrt(total_rows / scale) * jnp.einsum(
        "smk,smp->skp", inverse_root, projected, precision=exact_precision
    )
    elements = jnp.einsum(
        "smk,sml->skl", inverse_root, cross, precision=exact_precision
    ) / jnp.sqrt(scale)
    elements = elements.reshape(sector_count, vector_count, 2, vector_count).transpose(0, 2, 1, 3)
    return (basis, elements)


def solution(mesh):
    finer = Mesh(mesh.devices.reshape(4, 3, 2, 4, 8), ("row_0", "row_1", "row_2", "col_0", "col_1"))
    in_specs = (
        P(None, None, COL_ROW),
        P(None, ROW, COL, None, None),
        P(None, ROW, COL),
        P(None, ROW, COL, None, None),
        P(None, ROW, COL),
    )
    out_specs = (P(None, None, ROW_COL), P())
    return jax.shard_map(
        per_device, mesh=finer, in_specs=in_specs, out_specs=out_specs, check_vma=False
    )
```

profile of v0, /device:TPU:64, one launch (start us, length us, event | category | flops | bytes accessed | tf_op | source)
XLA Modules:
  0.0 143.8 jit_solution(12981848498656926019)
XLA Ops:
  0.7 0.8 broadcast_in_dim.5
  1.5 0.7 reshape.652
  2.2 12.2 %all-to-all-start = ((bf16[24,2,256]{2,1,0:T(2,128)(2,1)}), bf16[24,2,256]{2,1,0:T(2,128)(2,1)S(1)}, u32[]{:S(2)}, u32[]{:S(2)}) async-start(bf16[24,2,256]{2,1,0:T(2,128)(2,1)} %reshape.652), calls=%async_computation | async-start | bytes 49152 | tf_op jit(solution)/shard_map/all_to_all | solution.py:25
  14.6 5.6 %all-to-all-done = bf16[24,2,256]{2,1,0:T(2,128)(2,1)S(1)} async-done(((bf16[24,2,256]{2,1,0:T(2,128)(2,1)}), bf16[24,2,256]{2,1,0:T(2,128)(2,1)S(1)}, u32[]{:S(2)}, u32[]{:S(2)}) %all-to-all-start) | async-done | bytes 24608 | tf_op jit(solution)/shard_map/all_to_all | solution.py:25
  20.7 0.3 convolution_bitcast_fusion.1
  21.0 0.2 convolution_bitcast_fusion
  21.4 0.2 convolution_convert_fusion
  21.7 0.6 fusion.7
  22.3 0.3 convolution_bitcast_fusion.2
  22.8 0.5 copy.24
  23.3 0.5 reshape.654
  23.8 30.1 %all_to_all.10 = f32[32,1,1536]{2,1,0:T(1,128)S(1)} all-to-all(f32[32,1,1536]{2,1,0:T(1,128)S(1)} %reshape.654), channel_id=1, replica_groups=mesh['row_0'=4,'row_1'=3,'row_2'=2,'col_0'=4,'col_1'=8] {'col_0','col_1'}, dimensions={0} | all-to-all | bytes 393216 | tf_op jit(solution)/shard_map/all_to_all | solution.py:42
  53.9 0.5 broadcast.509
  54.4 1.1 reduce.2
  55.5 0.2 reshape.655
  55.8 0.2 convolution_bitcast_fusion.3
  56.2 15.2 %all-reduce.2 = (f32[1,16,16]{2,1,0:T(8,128)S(1)}, f32[1,16,32]{2,1,0:T(8,128)S(1)}) all-reduce(f32[1,16,16]{2,1,0:T(8,128)S(1)} %convolution_bitcast_fusion.4, f32[1,16,32]{2,1,0:T(8,128)S(1)} %convolution_bitcast_fusion.3), channel_id=1, replica_groups=mesh['row_0'=4,'row_1'=3,'row_2'=2,'col_0'=4,'col_1'=8] {'row_0'}, use_global_device_ids=true, to_apply=%region_1.2 | all-reduce | flops 768 | bytes 6144 | tf_op jit(solution)/shard_map/psum | solution.py:57
  71.5 11.8 %all-reduce.3 = (f32[1,16,16]{2,1,0:T(8,128)S(1)}, f32[1,16,32]{2,1,0:T(8,128)S(1)}) all-reduce(f32[1,16,16]{2,1,0:T(8,128)S(1)} %get-tuple-element.6, f32[1,16,32]{2,1,0:T(8,128)S(1)} %get-tuple-element.7), channel_id=1, replica_groups=mesh['row_0'=4,'row_1'=3,'row_2'=2,'col_0'=4,'col_1'=8] {'row_1'}, use_global_device_ids=true, to_apply=%region_2.3 | all-reduce | flops 768 | bytes 6144 | tf_op jit(solution)/shard_map/psum | solution.py:57
  83.3 3.3 %all-reduce.4 = (f32[1,16,16]{2,1,0:T(8,128)S(1)}, f32[1,16,32]{2,1,0:T(8,128)S(1)}) all-reduce(f32[1,16,16]{2,1,0:T(8,128)S(1)} %get-tuple-element.8, f32[1,16,32]{2,1,0:T(8,128)S(1)} %get-tuple-element.9), channel_id=1, replica_groups=mesh['row_0'=4,'row_1'=3,'row_2'=2,'col_0'=4,'col_1'=8] {'row_2'}, use_global_device_ids=true, to_apply=%region_3.4 | all-reduce | flops 768 | bytes 6144 | tf_op jit(solution)/shard_map/psum | solution.py:57
  86.5 24.0 %all-reduce.1 = (f32[1,16,16]{2,1,0:T(8,128)S(1)}, f32[1,16,32]{2,1,0:T(8,128)S(1)}) all-reduce(f32[1,16,16]{2,1,0:T(8,128)S(1)} %get-tuple-element.10, f32[1,16,32]{2,1,0:T(8,128)S(1)} %get-tuple-element.11), channel_id=1, replica_groups=mesh['row_0'=4,'row_1'=3,'row_2'=2,'col_0'=4,'col_1'=8] {'col_0'}, use_global_device_ids=true, to_apply=%region_4.5 | all-reduce | flops 768 | bytes 6144 | tf_op jit(solution)/shard_map/psum | solution.py:57
  110.6 27.7 %all-reduce = (f32[1,16,16]{2,1,0:T(8,128)S(1)}, f32[16,32]{1,0:T(8,128)S(1)}) all-reduce(f32[1,16,16]{2,1,0:T(8,128)S(1)} %get-tuple-element.4, f32[16,32]{1,0:T(8,128)S(1)} %bitcast.140), channel_id=1, replica_groups=mesh['row_0'=4,'row_1'=3,'row_2'=2,'col_0'=4,'col_1'=8] {'col_1'}, use_global_device_ids=true, to_apply=%region_5.6 | all-reduce | flops 768 | bytes 6144 | tf_op jit(solution)/shard_map/psum | solution.py:57
  138.3 0.6 multiply_reduce_fusion
  142.3 0.6 copy.38
  143.0 0.8 fusion
  (46 shorter events, 3.8 us)
Async XLA Ops:
  0.6 21.1 %copy-start = (bf16[1,1,32,128,128]{4,3,2,1,0:T(8,128)(2,1)S(1)}, bf16[1,1,32,128,128]{4,3,2,1,0:T(8,128)(2,1)}, u32[]{:S(2)}) copy-start(bf16[1,1,32,128,128]{4,3,2,1,0:T(8,128)(2,1)} %param.6) | copy-start | bytes 3145732
  0.6 13.7 %copy-start.2 = (s32[1,1,12]{2,1,0:T(1,128)S(1)}, s32[1,1,12]{2,1,0:T(1,128)}, u32[]{:S(2)}) copy-start(s32[1,1,12]{2,1,0:T(1,128)} %param.9) | copy-start | bytes 148
  0.7 13.8 %copy-start.3 = (s32[1,1,32]{2,1,0:T(1,128)S(1)}, s32[1,1,32]{2,1,0:T(1,128)}, u32[]{:S(2)}) copy-start(s32[1,1,32]{2,1,0:T(1,128)} %param.7) | copy-start | bytes 388
  1.5 19.2 %copy-start.1 = (bf16[1,1,12,128,128]{4,3,2,1,0:T(8,128)(2,1)S(1)}, bf16[1,1,12,128,128]{4,3,2,1,0:T(8,128)(2,1)}, u32[]{:S(2)}) copy-start(bf16[1,1,12,128,128]{4,3,2,1,0:T(8,128)(2,1)} %param.8) | copy-start | bytes 1179652
  2.2 18.0 %all-to-all-start = ((bf16[24,2,256]{2,1,0:T(2,128)(2,1)}), bf16[24,2,256]{2,1,0:T(2,128)(2,1)S(1)}, u32[]{:S(2)}, u32[]{:S(2)}) async-start(bf16[24,2,256]{2,1,0:T(2,128)(2,1)} %reshape.652), calls=%async_computation | async-start | bytes 49152 | tf_op jit(solution)/shard_map/all_to_all | solution.py:25
where the time goes:
time: 144 us
  blocking collectives  112 us (78%)
  starting transfers between devices  12.2 us (8%)
  matrix products  5.69 us (4%)
  waiting for transfers between devices  5.64 us (4%)
  local copies, waits for them, and re-layouts  4.47 us (3%)
  other arithmetic  1.93 us (1%)
  between operations  1.71 us (1%)
    psum x5, blocking collectives, over_axes(): value = lax.psum(value, axis)  82.1 us
    all_to_all x1, blocking collectives, sent_and_summed(): pieces = lax.all_to_all(split_up(value, dim, peers), axis, 0, 0, tiled=True)  30.1 us
    all_to_all x1, starting transfers between devices, sent_to_all(): lax.all_to_all(jnp.broadcast_to(value[None], (peers, *value.shape)), axis...  12.2 us
    all_to_all x1, waiting for transfers between devices, sent_to_all(): lax.all_to_all(jnp.broadcast_to(value[None], (peers, *value.shape)), axis...  5.64 us
  transfers between devices with their start and end apart: 1, of which 1 were waited for; matrix products, arithmetic and copies ran while one was open for 0% of the time, Pallas kernels for 0%

commit v1 on v0

v1 whole, which is shorter than its diff:
```python
import functools

import jax
import jax.numpy as jnp
from jax import lax
from jax.experimental import pallas as pl
from jax.experimental.pallas import tpu as pltpu
from jax.sharding import PartitionSpec as P

NSIT = 6
MESH = pl.DeviceIdType.MESH
F32 = jnp.float32
BF16 = jnp.bfloat16
NY = 8
NZ = 4
K = 16
T = 128
NT = (((1,), (1,)), ((), ()))


def iota(shape, dim):
    return lax.broadcasted_iota(jnp.int32, shape, dim)


def three_parts(x):
    a = x.astype(BF16).astype(F32)
    rest = x - a
    b = rest.astype(BF16).astype(F32)
    return a, b, rest - b


def small_dot(left, right, group):
    a1, a2, a3 = three_parts(left)
    b1, b2, b3 = (b.astype(BF16) for b in three_parts(right))
    lhs = jnp.where(
        (group == 0) | (group == 1) | (group == 4),
        a1,
        jnp.where((group == 5) | (group == 7), a3, a2),
    )
    rhs = jnp.concatenate([b1, b2, b1, b2, b3, b1, b3, b2], axis=0)
    return jnp.dot(lhs.astype(BF16), rhs, preferred_element_type=F32)


def long_dot(left, right):
    return lax.dot_general(
        left, right, NT, precision=lax.Precision.HIGHEST, preferred_element_type=F32
    )


def flat_rows(repeated):
    own = iota((8, T), 1) // K == iota((8, T), 0)
    return [
        jnp.sum(jnp.where(own, repeated[8 * h : 8 * h + 8], 0.0), axis=0, keepdims=True)
        for h in range(2)
    ]


def from_flat(rows):
    own = iota((8, T), 1) // K == iota((8, T), 0)
    full = jnp.concatenate(
        [jnp.where(own, jnp.broadcast_to(row, (8, T)), 0.0) for row in rows], axis=0
    )
    for shift in (64, 32, 16):
        full = full + pltpu.roll(full, shift, 1)
    return full


def kernel(
    n_row, n_col, total_rows,
    vec_hbm, ht_hbm, hl, jt_hbm, jl, basis_ref, elem_ref,
    vloc, vsend, vrecv, vblk, ht, jt, hs, hr, js, jr, zr, gs, ga, gb, cs, ca, cb, ps,
    lsem, ssem, rsem,
):
    me_r = lax.axis_index("row")
    me_c = lax.axis_index("col")
    zh = me_c // NY
    y = me_c % NY
    barrier = pltpu.get_barrier_semaphore()

    def at_row(d):
        return {"row": lax.rem(me_r + d, n_row)}

    def at_col(d):
        return {"col": lax.rem(me_c + d, n_col)}

    def at_y(d):
        return {"col": zh * NY + lax.rem(y + d, NY)}

    def at_z(d):
        return {"col": lax.rem(zh + d, NZ) * NY + y}

    loads = [
        pltpu.make_async_copy(vec_hbm, vloc, lsem.at[0]),
        pltpu.make_async_copy(ht_hbm, ht, lsem.at[1]),
        pltpu.make_async_copy(jt_hbm, jt, lsem.at[2]),
    ]
    for load in loads:
        load.start()

    def greet(where):
        def step(d, carry):
            pl.semaphore_signal(barrier, inc=1, device_id=where(d), device_id_type=MESH)
            return carry
        return step

    lax.fori_loop(1, n_row, greet(at_row), 0)
    lax.fori_loop(1, n_col, greet(at_col), 0)

    def send_all(at, where, count, src, dst):
        def step(d, carry):
            pltpu.make_async_remote_copy(
                src_ref=src(d), dst_ref=dst, send_sem=ssem.at[at], recv_sem=rsem.at[at],
                device_id=where(d), device_id_type=MESH,
            ).start()
            return carry
        lax.fori_loop(1, count, step, 0)

    def wait_for(sem, at, buf, count):
        part = buf.at[pl.ds(0, count)]
        pltpu.make_async_copy(part, part, sem.at[at]).wait()

    loads[0].wait()
    place = (iota((32, T), 1) == iota((32, T), 0) + 32 * lax.rem(me_r, 4)).astype(F32).astype(BF16)
    mine = jnp.dot(vloc[0], place, preferred_element_type=F32).astype(BF16)
    vsend[...] = mine
    vrecv[me_r] = mine

    pl.semaphore_wait(barrier, n_row + n_col - 2)
    send_all(0, at_row, n_row, lambda d: vsend, vrecv.at[me_r])
    loads[1].wait()
    loads[2].wait()
    wait_for(rsem, 0, vrecv, n_row - 1)

    for c in range(6):
        block = (vrecv[4 * c].astype(F32) + vrecv[4 * c + 1].astype(F32)) + (
            vrecv[4 * c + 2].astype(F32) + vrecv[4 * c + 3].astype(F32)
        )
        vblk[c] = block

    def masked(code, blocks):
        m = lax.shift_right_arithmetic(code * 43, 8)
        picked = vblk[code - 6 * m]
        which = jnp.full((K, T), m, jnp.int32)
        return jnp.concatenate(
            [jnp.where(which == b, picked, 0.0).astype(BF16) for b in range(blocks)], axis=0
        )

    def products(codes, tiles, count, blocks):
        total = jnp.zeros((blocks * K, T), F32)
        for q in range(0, count, 2):
            left = jnp.concatenate([masked(codes[q + e], blocks) for e in range(2)], axis=1)
            right = jnp.concatenate([tiles[q + e] for e in range(2)], axis=1)
            total = total + lax.dot_general(left, right, NT, preferred_element_type=F32)
        return total

    lane32 = iota((K, T), 1) // 32

    def packed(total, first, yh, s):
        out = None
        for z in range(NZ):
            at = (first + 2 * z + yh) * K
            piece = total[at : at + K]
            shift = ((z - s) % NZ) * 32
            if shift:
                piece = pltpu.roll(piece, shift, 1)
            out = piece if out is None else jnp.where(lane32 == z, piece, out)
        return out

    h_total = products(hl, ht, hl.shape[0], 8)
    for yh in range(2):
        for s in range(4):
            hs[yh * 4 + s] = packed(h_total, 0, yh, s)
    hr[y] = hs[y]
    send_all(1, at_y, NY, lambda d: hs.at[lax.rem(y + d, NY)], hr.at[y])

    j_total = products(jl, jt, jl.shape[0], 16)
    for yh in range(2):
        for s in range(4):
            for o in range(2):
                js[yh * 4 + s, o * K : o * K + K] = packed(j_total, o * 8, yh, s)
    jr[y] = js[y]
    send_all(2, at_y, NY, lambda d: js.at[lax.rem(y + d, NY)], jr.at[y])

    wait_for(rsem, 1, hr, NY - 1)
    part = hr[0]
    for d in range(1, NY):
        part = part + hr[d]
    zr[zh] = part
    send_all(3, at_z, NZ, lambda d: zr.at[zh], zr.at[zh])
    wait_for(rsem, 3, zr, NZ - 1)
    proj = (zr[0] + zr[1]) + (zr[2] + zr[3])

    rows = flat_rows(long_dot(proj, jnp.concatenate([proj] * 8, axis=0)))
    for h in range(2):
        gs[h : h + 1] = rows[h]
        ga[y, h : h + 1] = rows[h]
    send_all(4, at_y, NY, lambda d: gs, ga.at[y])
    own_lanes = proj
    for z in range(1, NZ):
        own_lanes = jnp.where(jnp.full((K, T), zh, jnp.int32) == z, pltpu.roll(proj, (NZ - z) * 32, 1), own_lanes)
    ps[...] = own_lanes

    wait_for(rsem, 2, jr, NY - 1)
    share = jr[0]
    for d in range(1, NY):
        share = share + jr[d]
    for o in range(2):
        rows = flat_rows(long_dot(proj, jnp.concatenate([share[o * K : o * K + K]] * 8, axis=0)))
        for h in range(2):
            cs[2 * o + h : 2 * o + h + 1] = rows[h]
            ca[me_c, 2 * o + h : 2 * o + h + 1] = rows[h]
    send_all(5, at_col, n_col, lambda d: cs, ca.at[me_c])

    wait_for(rsem, 4, ga, NY - 1)
    part = ga[0]
    for d in range(1, NY):
        part = part + ga[d]
    gb[me_r] = part
    send_all(6, at_row, n_row, lambda d: gb.at[me_r], gb.at[me_r])

    wait_for(rsem, 5, ca, n_col - 1)
    part = ca[0]
    for d in range(1, n_col):
        part = part + ca[d]
    cb[me_r] = part
    send_all(7, at_row, n_row, lambda d: cb.at[me_r], cb.at[me_r])

    wait_for(rsem, 6, gb, n_row - 1)
    part = gb[0]
    for d in range(1, n_row):
        part = part + gb[d]
    square = jnp.sum(jnp.sum(part * part, axis=1, keepdims=True), axis=0, keepdims=True)
    scale = jnp.sqrt(jnp.broadcast_to(square, (K, T)) + 1e-06)
    iterate = from_flat([part[0:1], part[1:2]]) / scale
    group = iota((K, T), 1) // K
    identity = (iota((K, T), 1) % K == iota((K, T), 0)).astype(F32)
    middle = 1.5 * identity - 0.5 * iterate
    iterate = small_dot(middle, iterate, group)
    root = middle
    for step in range(1, NSIT):
        middle = 1.5 * identity - 0.5 * small_dot(iterate, root, group)
        if step < NSIT - 1:
            iterate = small_dot(middle, iterate, group)
        root = small_dot(root, middle, group)
    basis = jnp.sqrt(total_rows / scale) * small_dot(root, ps[...], group)
    basis_ref[0] = basis[:, :32]

    wait_for(rsem, 7, cb, n_row - 1)
    part = cb[0]
    for d in range(1, n_row):
        part = part + cb[d]
    for o in range(2):
        cross = from_flat([part[2 * o : 2 * o + 1], part[2 * o + 1 : 2 * o + 2]])
        elements = small_dot(root, cross, group) / jnp.sqrt(scale)
        elem_ref[0, o] = elements[:, :K]

    wait_for(ssem, 0, vrecv, n_row - 1)
    wait_for(ssem, 1, hr, NY - 1)
    wait_for(ssem, 2, jr, NY - 1)
    wait_for(ssem, 3, zr, NZ - 1)
    wait_for(ssem, 4, ga, NY - 1)
    wait_for(ssem, 5, ca, n_col - 1)
    wait_for(ssem, 6, gb, n_row - 1)
    wait_for(ssem, 7, cb, n_row - 1)


def solution(mesh):
    n_row, n_col = mesh.shape["row"], mesh.shape["col"]

    def per_device(vectors, h_tiles, h_list, j_tiles, j_list):
        hq, jq = h_tiles.shape[2], j_tiles.shape[2]
        total_rows = vectors.shape[2] * n_row * n_col
        hbm = pl.BlockSpec(memory_space=pl.ANY)
        smem = pl.BlockSpec(memory_space=pltpu.SMEM)
        vmem = pl.BlockSpec(memory_space=pltpu.VMEM)
        return pl.pallas_call(
            functools.partial(kernel, n_row, n_col, float(total_rows)),
            out_shape=(
                jax.ShapeDtypeStruct((1, K, 32), F32),
                jax.ShapeDtypeStruct((1, 2, K, K), F32),
            ),
            in_specs=[hbm, hbm, smem, hbm, smem],
            out_specs=(vmem, vmem),
            scratch_shapes=[
                pltpu.VMEM((1, K, 32), BF16),
                pltpu.VMEM((K, T), BF16),
                pltpu.VMEM((n_row, K, T), BF16),
                pltpu.VMEM((6, K, T), F32),
                pltpu.VMEM((hq, T, T), BF16),
                pltpu.VMEM((jq, T, T), BF16),
                pltpu.VMEM((NY, K, T), F32),
                pltpu.VMEM((NY, K, T), F32),
                pltpu.VMEM((NY, 2 * K, T), F32),
                pltpu.VMEM((NY, 2 * K, T), F32),
                pltpu.VMEM((NZ, K, T), F32),
                pltpu.VMEM((2, T), F32),
                pltpu.VMEM((NY, 2, T), F32),
                pltpu.VMEM((n_row, 2, T), F32),
                pltpu.VMEM((4, T), F32),
                pltpu.VMEM((n_col, 4, T), F32),
                pltpu.VMEM((n_row, 4, T), F32),
                pltpu.VMEM((K, T), F32),
                pltpu.SemaphoreType.DMA((3,)),
                pltpu.SemaphoreType.DMA((8,)),
                pltpu.SemaphoreType.DMA((8,)),
            ],
            compiler_params=pltpu.CompilerParams(
                collective_id=0, has_side_effects=True, vmem_limit_bytes=24 * 1024 * 1024
            ),
        )(
            vectors,
            h_tiles.reshape(hq, T, T),
            h_list.reshape(hq),
            j_tiles.reshape(jq, T, T),
            j_list.reshape(jq),
        )

    return jax.shard_map(
        per_device,
        mesh=mesh,
        in_specs=(
            P(None, None, ("col", "row")),
            P(None, "row", "col", None, None),
            P(None, "row", "col"),
            P(None, "row", "col", None, None),
            P(None, "row", "col"),
        ),
        out_specs=(P(None, None, ("row", "col")), P()),
        check_vma=False,
    )
```

time: 144 us -> 59 us (0.41)
  the two profiles are of different devices: /device:TPU:64 before, /device:TPU:1 now
where the time goes in v1:
time: 59 us; the launch traced here: 58.8 us
  Pallas kernels  54 us (92%)
  local copies, waits for them, and re-layouts  4.09 us (7%)
  between operations  0.67 us (1%)
    pallas_call x1, Pallas kernels, per_device(): pl.pallas_call(functools.partial(kernel, n_row, n_col, float(total_rows))...  54 us
    unnamed x12, local copies, waits for them, and re-layouts  4.09 us

profile of v1, /device:TPU:1, one launch (start us, length us, event | category | flops | bytes accessed | tf_op | source)
XLA Modules:
  0.0 58.8 jit_solution(5406499458432191976)
XLA Ops:
  0.6 0.0 copy-start.2
  0.6 0.0 copy-start.3
  0.7 0.0 copy-start.4
  0.7 0.7 %copy-done.2 = bf16[1,16,32]{2,1,0:T(8,128)(2,1)S(1)} copy-done((bf16[1,16,32]{2,1,0:T(8,128)(2,1)S(1)}, bf16[1,16,32]{2,1,0:T(8,128)(2,1)}, u32[]{:S(2)}) %copy-start.2) | copy-done | bytes 1048
  1.3 0.0 copy-done.3
  1.3 0.0 copy-done.4
  1.3 0.0 copy-start
  1.3 1.2 %copy-done = bf16[1,1,32,128,128]{4,3,2,1,0:T(8,128)(2,1)S(1)} copy-done((bf16[1,1,32,128,128]{4,3,2,1,0:T(8,128)(2,1)S(1)}, bf16[1,1,32,128,128]{4,3,2,1,0:T(8,128)(2,1)}, u32[]{:S(2)}) %copy-start) | copy-done | bytes 1048600
  2.6 0.0 copy-start.1
  2.6 1.0 %copy-done.1 = bf16[1,1,12,128,128]{4,3,2,1,0:T(8,128)(2,1)S(1)} copy-done((bf16[1,1,12,128,128]{4,3,2,1,0:T(8,128)(2,1)S(1)}, bf16[1,1,12,128,128]{4,3,2,1,0:T(8,128)(2,1)}, u32[]{:S(2)}) %copy-start.1) | copy-done | bytes 393240
  3.5 54.0 %shard_map.68 = (f32[1,16,32]{2,1,0:T(8,128)S(1)}, f32[1,2,16,16]{3,2,1,0:T(8,128)S(1)}) custom-call(bf16[1,16,32]{2,1,0:T(8,128)(2,1)S(1)} %copy-done.2, bf16[32,128,128]{2,1,0:T(8,128)(2,1)S(1)} %bitcast.4, s32[32]{0:T(128)S(1)} %bitcast.6, bf16[12,128,128]{2,1,0:T(8,128)(2,1)S(1)} %bitcast.5, s32[12]{0:T(128)S(1)} %bitcast.7), custom_call_target="tpu_custom_call" | custom-call | tf_op jit(solution)/shard_map/pallas_call | solution.py:276
  57.6 0.6 %copy.9 = f32[1,16,32]{2,1,0:T(8,128)} copy(f32[1,16,32]{2,1,0:T(8,128)S(1)} %get-tuple-element.4) | data formatting | bytes 4096
  58.2 0.6 %copy.10 = f32[1,2,16,16]{3,2,1,0:T(8,128)} copy(f32[1,2,16,16]{3,2,1,0:T(8,128)S(1)} %get-tuple-element.5) | data formatting | bytes 4096
Async XLA Ops:
  0.6 0.7 %copy-start.2 = (bf16[1,16,32]{2,1,0:T(8,128)(2,1)S(1)}, bf16[1,16,32]{2,1,0:T(8,128)(2,1)}, u32[]{:S(2)}) copy-start(bf16[1,16,32]{2,1,0:T(8,128)(2,1)} %vec_hbm.1) | copy-start | bytes 3076
  0.6 0.7 %copy-start.3 = (s32[1,1,32]{2,1,0:T(1,128)S(1)}, s32[1,1,32]{2,1,0:T(1,128)}, u32[]{:S(2)}) copy-start(s32[1,1,32]{2,1,0:T(1,128)} %param.7) | copy-start | bytes 388
  0.7 0.7 %copy-start.4 = (s32[1,1,12]{2,1,0:T(1,128)S(1)}, s32[1,1,12]{2,1,0:T(1,128)}, u32[]{:S(2)}) copy-start(s32[1,1,12]{2,1,0:T(1,128)} %param.9) | copy-start | bytes 148
  1.3 1.2 %copy-start = (bf16[1,1,32,128,128]{4,3,2,1,0:T(8,128)(2,1)S(1)}, bf16[1,1,32,128,128]{4,3,2,1,0:T(8,128)(2,1)}, u32[]{:S(2)}) copy-start(bf16[1,1,32,128,128]{4,3,2,1,0:T(8,128)(2,1)} %param.6) | copy-start | bytes 3145732
  2.6 1.0 %copy-start.1 = (bf16[1,1,12,128,128]{4,3,2,1,0:T(8,128)(2,1)S(1)}, bf16[1,1,12,128,128]{4,3,2,1,0:T(8,128)(2,1)}, u32[]{:S(2)}) copy-start(bf16[1,1,12,128,128]{4,3,2,1,0:T(8,128)(2,1)} %param.8) | copy-start | bytes 1179652

commit v2 on v1

v2 whole, which is shorter than its diff:
```python
import functools

import jax
import jax.numpy as jnp
from jax import lax
from jax.experimental import pallas as pl
from jax.experimental.pallas import tpu as pltpu
from jax.sharding import PartitionSpec as P

NSIT = 6
MESH = pl.DeviceIdType.MESH
F32 = jnp.float32
BF16 = jnp.bfloat16
NY = 8
NZ = 4
NX = 4
VEC, HY, JY, HZ, JZ, PZ, GA, CA, GB, CB = range(10)
K = 16
T = 128
NT = (((1,), (1,)), ((), ()))


def iota(shape, dim):
    return lax.broadcasted_iota(jnp.int32, shape, dim)


def three_parts(x):
    a = x.astype(BF16).astype(F32)
    rest = x - a
    b = rest.astype(BF16).astype(F32)
    return a, b, rest - b


def small_dot(left, right, group):
    a1, a2, a3 = three_parts(left)
    b1, b2, b3 = (b.astype(BF16) for b in three_parts(right))
    lhs = jnp.where(
        (group == 0) | (group == 1) | (group == 4),
        a1,
        jnp.where((group == 5) | (group == 7), a3, a2),
    )
    rhs = jnp.concatenate([b1, b2, b1, b2, b3, b1, b3, b2], axis=0)
    return jnp.dot(lhs.astype(BF16), rhs, preferred_element_type=F32)


def long_dot(left, right):
    return lax.dot_general(
        left, right, NT, precision=lax.Precision.HIGHEST, preferred_element_type=F32
    )


def flat_rows(repeated):
    own = iota((8, T), 1) // K == iota((8, T), 0)
    return [
        jnp.sum(jnp.where(own, repeated[8 * h : 8 * h + 8], 0.0), axis=0, keepdims=True)
        for h in range(2)
    ]


def from_flat(rows):
    own = iota((8, T), 1) // K == iota((8, T), 0)
    full = jnp.concatenate(
        [jnp.where(own, jnp.broadcast_to(row, (8, T)), 0.0) for row in rows], axis=0
    )
    for shift in (64, 32, 16):
        full = full + pltpu.roll(full, shift, 1)
    return full


def kernel(
    n_row, n_col, total_rows,
    vec_hbm, ht_hbm, hl_hbm, jt_hbm, jl_hbm, basis_ref, elem_ref,
    vloc, vsend, vrecv, vblk, ht, jt, hl, jl, hs, hr, js, jr, hz, jz, pz, gs, ga, gb, cs, ca, cb,
    lsem, ssem, rsem,
):
    me_r = lax.axis_index("row")
    me_c = lax.axis_index("col")
    zh = me_c // NY
    y = me_c % NY
    x = me_r // (n_row // NX)
    inner = me_r % (n_row // NX)
    n_in = n_row // NX
    last = NZ - 1
    at_last = zh == last
    barrier = pltpu.get_barrier_semaphore()

    def wrap(value, count):
        return jnp.where(value >= count, value - count, value)

    def at_row(d):
        return {"row": wrap(me_r + d, n_row)}

    def at_y(d):
        return {"col": zh * NY + wrap(y + d, NY)}

    def at_z(d):
        return {"col": wrap(zh + d, NZ) * NY + y}

    def at_plane(d):
        to = y * NX + x + d
        to = wrap(to, NX * NY)
        return {"row": (to % NX) * n_in + inner, "col": zh * NY + to // NX}

    def at_line(d):
        to = wrap(zh * n_in + inner + d, NZ * n_in)
        return {"row": x * n_in + to % n_in, "col": (to // n_in) * NY + y}

    def at_collector(d):
        return {"col": last * NY + y}

    codes = [
        pltpu.make_async_copy(hl_hbm, hl, lsem.at[3]),
        pltpu.make_async_copy(jl_hbm, jl, lsem.at[4]),
    ]
    loads = [
        pltpu.make_async_copy(vec_hbm, vloc, lsem.at[0]),
        pltpu.make_async_copy(ht_hbm, ht, lsem.at[1]),
        pltpu.make_async_copy(jt_hbm, jt, lsem.at[2]),
    ]

    def greet(where):
        def step(d, carry):
            pl.semaphore_signal(barrier, inc=1, device_id=where(d), device_id_type=MESH)
            return carry
        return step

    def send_all(at, where, count, src, dst):
        def step(d, carry):
            pltpu.make_async_remote_copy(
                src_ref=src(d), dst_ref=dst, send_sem=ssem.at[at], recv_sem=rsem.at[at],
                device_id=where(d), device_id_type=MESH,
            ).start()
            return carry
        lax.fori_loop(1, count + 1, step, 0)

    def wait_for(sem, at, buf, count):
        part = buf.at[pl.ds(0, count)]
        pltpu.make_async_copy(part, part, sem.at[at]).wait()

    def total_of(buf, count):
        parts = [buf[d] for d in range(count)]
        while len(parts) > 1:
            parts = [sum(parts[k + 1 : k + 2], parts[k]) for k in range(0, len(parts), 2)]
        return parts[0]

    lax.fori_loop(1, n_row, greet(at_row), 0)
    lax.fori_loop(1, NY, greet(at_y), 0)
    lax.fori_loop(1, NZ, greet(at_z), 0)
    for load in [loads[0]] + codes + loads[1:]:
        load.start()
    loads[0].wait()
    place = (iota((32, T), 1) == iota((32, T), 0) + 32 * lax.rem(me_r, 4)).astype(F32).astype(BF16)
    mine = jnp.dot(vloc[0], place, preferred_element_type=F32).astype(BF16)
    vsend[...] = mine
    vrecv[me_r] = mine
    for load in codes:
        load.wait()

    pl.semaphore_wait(barrier, n_row - 1 + NY - 1 + NZ - 1)
    send_all(VEC, at_row, n_row - 1, lambda d: vsend, vrecv.at[me_r])
    loads[1].wait()
    loads[2].wait()
    wait_for(rsem, VEC, vrecv, n_row - 1)

    for c in range(6):
        block = (vrecv[4 * c].astype(F32) + vrecv[4 * c + 1].astype(F32)) + (
            vrecv[4 * c + 2].astype(F32) + vrecv[4 * c + 3].astype(F32)
        )
        vblk[c] = block

    def masked(code, blocks):
        m = lax.shift_right_arithmetic(code * 43, 8)
        picked = vblk[code - 6 * m]
        which = jnp.full((K, T), m, jnp.int32)
        return jnp.concatenate(
            [jnp.where(which == b, picked, 0.0).astype(BF16) for b in range(blocks)], axis=0
        )

    def products(codes, tiles, count, blocks):
        total = jnp.zeros((blocks * K, T), F32)
        for q in range(0, count, 2):
            left = jnp.concatenate([masked(codes[0, 0, q + e], blocks) for e in range(2)], axis=1)
            right = jnp.concatenate([tiles[q + e] for e in range(2)], axis=1)
            total = total + lax.dot_general(left, right, NT, preferred_element_type=F32)
        return total

    lane32 = iota((K, T), 1) // 32

    def packed(total, first, yh, s):
        out = None
        for z in range(NZ):
            at = (first + 2 * z + yh) * K
            piece = total[at : at + K]
            shift = ((z - s) % NZ) * 32
            if shift:
                piece = pltpu.roll(piece, shift, 1)
            out = piece if out is None else jnp.where(lane32 == z, piece, out)
        return out

    h_total = products(hl, ht, ht.shape[0], 8)
    for yh in range(2):
        for s in range(4):
            hs[yh * 4 + s] = packed(h_total, 0, yh, s)
    hr[y] = hs[y]
    send_all(HY, at_y, NY - 1, lambda d: hs.at[wrap(y + d, NY)], hr.at[y])

    j_total = products(jl, jt, jt.shape[0], 16)
    for yh in range(2):
        for s in range(4):
            for o in range(2):
                js[yh * 4 + s, o * K : o * K + K] = packed(j_total, o * 8, yh, s)
    jr[y] = js[y]
    send_all(JY, at_y, NY - 1, lambda d: js.at[wrap(y + d, NY)], jr.at[y])

    wait_for(rsem, HY, hr, NY - 1)
    hz[zh] = total_of(hr, NY)

    @pl.when(jnp.logical_not(at_last))
    def _():
        send_all(HZ, at_collector, 1, lambda d: hz.at[zh], hz.at[zh])
        wait_for(rsem, JY, jr, NY - 1)
        jz[zh] = total_of(jr, NY)
        send_all(JZ, at_collector, 1, lambda d: jz.at[zh], jz.at[zh])
        wait_for(rsem, PZ, pz, 1)

    @pl.when(at_last)
    def _():
        slot = y * NX + x
        wait_for(rsem, HZ, hz, NZ - 1)
        proj = total_of(hz, NZ)
        pz[0] = proj
        rows = flat_rows(long_dot(proj, jnp.concatenate([proj] * 8, axis=0)))
        for h in range(2):
            gs[h : h + 1] = rows[h]
            ga[slot, h : h + 1] = rows[h]
        send_all(GA, at_plane, NX * NY - 1, lambda d: gs, ga.at[slot])
        send_all(PZ, at_z, NZ - 1, lambda d: pz.at[0], pz.at[0])

        wait_for(rsem, JY, jr, NY - 1)
        jz[zh] = total_of(jr, NY)
        wait_for(rsem, JZ, jz, NZ - 1)
        share = total_of(jz, NZ)
        for o in range(2):
            rows = flat_rows(
                long_dot(proj, jnp.concatenate([share[o * K : o * K + K]] * 8, axis=0))
            )
            for h in range(2):
                cs[2 * o + h : 2 * o + h + 1] = rows[h]
                ca[slot, 2 * o + h : 2 * o + h + 1] = rows[h]
        send_all(CA, at_plane, NX * NY - 1, lambda d: cs, ca.at[slot])

        wait_for(rsem, GA, ga, NX * NY - 1)
        gb[inner] = total_of(ga, NX * NY)
        send_all(GB, at_line, NZ * n_in - 1, lambda d: gb.at[inner], gb.at[inner])
        wait_for(rsem, CA, ca, NX * NY - 1)
        cb[inner] = total_of(ca, NX * NY)
        send_all(CB, at_line, NZ * n_in - 1, lambda d: cb.at[inner], cb.at[inner])
        wait_for(rsem, GB, gb, n_in - 1)

    @pl.when(jnp.logical_not(at_last))
    def _():
        wait_for(rsem, GB, gb, n_in)

    part = total_of(gb, n_in)
    square = jnp.sum(jnp.sum(part * part, axis=1, keepdims=True), axis=0, keepdims=True)
    scale = jnp.sqrt(jnp.broadcast_to(square, (K, T)) + 1e-06)
    iterate = from_flat([part[0:1], part[1:2]]) / scale
    group = iota((K, T), 1) // K
    identity = (iota((K, T), 1) % K == iota((K, T), 0)).astype(F32)
    middle = 1.5 * identity - 0.5 * iterate
    iterate = small_dot(middle, iterate, group)
    root = middle
    for step in range(1, NSIT):
        middle = 1.5 * identity - 0.5 * small_dot(iterate, root, group)
        if step < NSIT - 1:
            iterate = small_dot(middle, iterate, group)
        root = small_dot(root, middle, group)
    basis = jnp.sqrt(total_rows / scale) * small_dot(root, pz[0], group)
    own_lanes = basis
    for z in range(1, NZ):
        own_lanes = jnp.where(
            jnp.full((K, T), zh, jnp.int32) == z, pltpu.roll(basis, (NZ - z) * 32, 1), own_lanes
        )
    basis_ref[0] = own_lanes[:, :32]

    @pl.when(jnp.logical_not(at_last))
    def _():
        wait_for(rsem, CB, cb, n_in)
        wait_for(ssem, HZ, hz, 1)
        wait_for(ssem, JZ, jz, 1)

    @pl.when(at_last)
    def _():
        wait_for(rsem, CB, cb, n_in - 1)
        wait_for(ssem, GA, ga, NX * NY - 1)
        for _ in range(NZ - 1):
            wait_for(ssem, PZ, pz, 1)
        wait_for(ssem, CA, ca, NX * NY - 1)
        for at, buf in ((GB, gb), (CB, cb)):
            for _ in range(NZ - 1):
                wait_for(ssem, at, buf, n_in)
            wait_for(ssem, at, buf, n_in - 1)

    part = total_of(cb, n_in)
    for o in range(2):
        cross = from_flat([part[2 * o : 2 * o + 1], part[2 * o + 1 : 2 * o + 2]])
        elements = small_dot(root, cross, group) / jnp.sqrt(scale)
        elem_ref[0, o] = elements[:, :K]
    wait_for(ssem, VEC, vrecv, n_row - 1)
    wait_for(ssem, HY, hr, NY - 1)
    wait_for(ssem, JY, jr, NY - 1)


def solution(mesh):
    n_row, n_col = mesh.shape["row"], mesh.shape["col"]

    def per_device(vectors, h_tiles, h_list, j_tiles, j_list):
        hq, jq = h_tiles.shape[2], j_tiles.shape[2]
        total_rows = vectors.shape[2] * n_row * n_col
        hbm = pl.BlockSpec(memory_space=pltpu.HBM)
        vmem = pl.BlockSpec(memory_space=pltpu.VMEM)
        return pl.pallas_call(
            functools.partial(kernel, n_row, n_col, float(total_rows)),
            out_shape=(
                jax.ShapeDtypeStruct((1, K, 32), F32),
                jax.ShapeDtypeStruct((1, 2, K, K), F32),
            ),
            in_specs=[hbm] * 5,
            out_specs=(vmem, vmem),
            scratch_shapes=[
                pltpu.VMEM((1, K, 32), BF16),
                pltpu.VMEM((K, T), BF16),
                pltpu.VMEM((n_row, K, T), BF16),
                pltpu.VMEM((6, K, T), F32),
                pltpu.VMEM((hq, T, T), BF16),
                pltpu.VMEM((jq, T, T), BF16),
                pltpu.SMEM((1, 1, hq), jnp.int32),
                pltpu.SMEM((1, 1, jq), jnp.int32),
                pltpu.VMEM((NY, K, T), F32),
                pltpu.VMEM((NY, K, T), F32),
                pltpu.VMEM((NY, 2 * K, T), F32),
                pltpu.VMEM((NY, 2 * K, T), F32),
                pltpu.VMEM((NZ, K, T), F32),
                pltpu.VMEM((NZ, 2 * K, T), F32),
                pltpu.VMEM((1, K, T), F32),
                pltpu.VMEM((2, T), F32),
                pltpu.VMEM((NX * NY, 2, T), F32),
                pltpu.VMEM((n_row // NX, 2, T), F32),
                pltpu.VMEM((4, T), F32),
                pltpu.VMEM((NX * NY, 4, T), F32),
                pltpu.VMEM((n_row // NX, 4, T), F32),
                pltpu.SemaphoreType.DMA((5,)),
                pltpu.SemaphoreType.DMA((10,)),
                pltpu.SemaphoreType.DMA((10,)),
            ],
            compiler_params=pltpu.CompilerParams(
                collective_id=0, has_side_effects=True, vmem_limit_bytes=60 * 1024 * 1024
            ),
        )(
            vectors,
            h_tiles.reshape(hq, T, T),
            h_list,
            j_tiles.reshape(jq, T, T),
            j_list,
        )

    return jax.shard_map(
        per_device,
        mesh=mesh,
        in_specs=(
            P(None, None, ("col", "row")),
            P(None, "row", "col", None, None),
            P(None, "row", "col"),
            P(None, "row", "col", None, None),
            P(None, "row", "col"),
        ),
        out_specs=(P(None, None, ("row", "col")), P()),
        check_vma=False,
    )
```

time: 59 us -> 52.8 us (0.89)
  Pallas kernels: 54 us -> 50 us
  local copies, waits for them, and re-layouts: 4.09 us -> 1.91 us
    pallas_call x1, Pallas kernels: 54 us -> 50 us  [per_device(): pl.pallas_call(functools.partial(kernel, n_row, n_col, float(total_rows))...]
    unnamed x12 -> x4, local copies, waits for them, and re-layouts: 4.09 us -> 1.91 us
where the time goes in v2:
time: 52.8 us; the launch traced here: 52.6 us
  Pallas kernels  50 us (95%)
  local copies, waits for them, and re-layouts  1.91 us (4%)
  between operations  0.65 us (1%)
    pallas_call x1, Pallas kernels, per_device(): pl.pallas_call(functools.partial(kernel, n_row, n_col, float(total_rows))...  50 us
    unnamed x4, local copies, waits for them, and re-layouts  1.91 us

profile of v2, /device:TPU:1, one launch (start us, length us, event | category | flops | bytes accessed | tf_op | source)
XLA Modules:
  0.0 52.6 jit_solution(5034384012254347163)
XLA Ops:
  0.6 50.0 %shard_map.68 = (f32[1,16,32]{2,1,0:T(8,128)}, f32[1,2,16,16]{3,2,1,0:T(8,128)}) custom-call(bf16[1,16,32]{2,1,0:T(8,128)(2,1)} %vec_hbm.1, bf16[32,128,128]{2,1,0:T(8,128)(2,1)} %bitcast.2, s32[1,1,32]{2,1,0:T(1,128)} %hl_hbm.1, bf16[12,128,128]{2,1,0:T(8,128)(2,1)} %bitcast.3, s32[1,1,12]{2,1,0:T(1,128)} %jl_hbm.1), custom_call_target="tpu_custom_call" | custom-call | tf_op jit(solution)/shard_map/pallas_call | solution.py:322
  50.6 0.0 copy-start
  50.6 1.3 %copy.9 = f32[1,16,32]{2,1,0:T(8,128)} copy(f32[1,16,32]{2,1,0:T(8,128)} %get-tuple-element.4) | data formatting | bytes 4096
  51.9 0.0 copy-done
  51.9 0.6 %copy.10 = f32[1,2,16,16]{3,2,1,0:T(8,128)} copy(f32[1,2,16,16]{3,2,1,0:T(8,128)S(1)} %copy-done) | data formatting | bytes 4096
Async XLA Ops:
  50.6 1.3 %copy-start = (f32[1,2,16,16]{3,2,1,0:T(8,128)S(1)}, f32[1,2,16,16]{3,2,1,0:T(8,128)}, u32[]{:S(2)}) copy-start(f32[1,2,16,16]{3,2,1,0:T(8,128)} %get-tuple-element.5) | copy-start | bytes 6148

commit v3 on v2

--- a/solution.py
+++ b/solution.py
@@ -14,7 +14,7 @@
 NY = 8
 NZ = 4
 NX = 4
-VEC, HY, JY, HZ, JZ, PZ, GA, CA, GB, CB = range(10)
+VEC, HY, JY, HZ, JZ, PZ, GA, CA, GB, CB, HU, JU = range(12)
 K = 16
 T = 128
 NT = (((1,), (1,)), ((), ()))
@@ -49,6 +49,36 @@
     )
 
 
+def coded(piece, first):
+    top = jnp.max(jnp.abs(piece), axis=1, keepdims=True)
+    unit = (jnp.maximum(top, 1e-30) * (1.01 / 32767)).astype(BF16).astype(F32)
+    steps = piece * jnp.broadcast_to(1.0 / unit, (K, T))
+    steps = (steps + jnp.where(steps >= 0, 0.5, -0.5)).astype(jnp.int32).astype(jnp.int16)
+    place = iota((K, T), 1) == iota((K, T), 0) + first
+    units = jnp.sum(
+        jnp.where(place, jnp.broadcast_to(unit, (K, T)), 0.0), axis=0, keepdims=True
+    )
+    return steps, units
+
+
+def decoded_total(steps, units, rows):
+    own = iota((rows, T), 1) == iota((rows, T), 0)
+    spread = jnp.concatenate(
+        [
+            jnp.where(own, jnp.broadcast_to(units[d], (rows, T)), 0.0).astype(BF16)
+            for d in range(NY)
+        ],
+        axis=0,
+    )
+    unit = jnp.dot(spread, jnp.ones((T, T), BF16), preferred_element_type=F32)
+    parts = [
+        steps[d].astype(jnp.int32).astype(F32) * unit[d * rows : (d + 1) * rows] for d in range(NY)
+    ]
+    while len(parts) > 1:
+        parts = [parts[k] + parts[k + 1] for k in range(0, len(parts), 2)]
+    return parts[0]
+
+
 def flat_rows(repeated):
     own = iota((8, T), 1) // K == iota((8, T), 0)
     return [
@@ -70,7 +100,7 @@
 def kernel(
     n_row, n_col, total_rows,
     vec_hbm, ht_hbm, hl_hbm, jt_hbm, jl_hbm, basis_ref, elem_ref,
-    vloc, vsend, vrecv, vblk, ht, jt, hl, jl, hs, hr, js, jr, hz, jz, pz, gs, ga, gb, cs, ca, cb,
+    vloc, vsend, vrecv, vblk, ht, jt, hl, jl, hs, hr, js, jr, hsu, hru, jsu, jru, hz, jz, pz, gs, ga, gb, cs, ca, cb,
     lsem, ssem, rsem,
 ):
     me_r = lax.axis_index("row")
@@ -200,26 +230,35 @@
     h_total = products(hl, ht, ht.shape[0], 8)
     for yh in range(2):
         for s in range(4):
-            hs[yh * 4 + s] = packed(h_total, 0, yh, s)
+            hs[yh * 4 + s], hsu[yh * 4 + s] = coded(packed(h_total, 0, yh, s), 0)
     hr[y] = hs[y]
+    hru[y] = hsu[y]
+    send_all(HU, at_y, NY - 1, lambda d: hsu.at[wrap(y + d, NY)], hru.at[y])
     send_all(HY, at_y, NY - 1, lambda d: hs.at[wrap(y + d, NY)], hr.at[y])
 
     j_total = products(jl, jt, jt.shape[0], 16)
     for yh in range(2):
         for s in range(4):
-            for o in range(2):
-                js[yh * 4 + s, o * K : o * K + K] = packed(j_total, o * 8, yh, s)
+            first, first_units = coded(packed(j_total, 0, yh, s), 0)
+            second, second_units = coded(packed(j_total, 8, yh, s), K)
+            js[yh * 4 + s, :K] = first
+            js[yh * 4 + s, K:] = second
+            jsu[yh * 4 + s] = first_units + second_units
     jr[y] = js[y]
+    jru[y] = jsu[y]
+    send_all(JU, at_y, NY - 1, lambda d: jsu.at[wrap(y + d, NY)], jru.at[y])
     send_all(JY, at_y, NY - 1, lambda d: js.at[wrap(y + d, NY)], jr.at[y])
 
+    wait_for(rsem, HU, hru, NY - 1)
     wait_for(rsem, HY, hr, NY - 1)
-    hz[zh] = total_of(hr, NY)
+    hz[zh] = decoded_total(hr, hru, K)
 
     @pl.when(jnp.logical_not(at_last))
     def _():
         send_all(HZ, at_collector, 1, lambda d: hz.at[zh], hz.at[zh])
+        wait_for(rsem, JU, jru, NY - 1)
         wait_for(rsem, JY, jr, NY - 1)
-        jz[zh] = total_of(jr, NY)
+        jz[zh] = decoded_total(jr, jru, 2 * K)
         send_all(JZ, at_collector, 1, lambda d: jz.at[zh], jz.at[zh])
         wait_for(rsem, PZ, pz, 1)
 
@@ -236,8 +275,9 @@
         send_all(GA, at_plane, NX * NY - 1, lambda d: gs, ga.at[slot])
         send_all(PZ, at_z, NZ - 1, lambda d: pz.at[0], pz.at[0])
 
+        wait_for(rsem, JU, jru, NY - 1)
         wait_for(rsem, JY, jr, NY - 1)
-        jz[zh] = total_of(jr, NY)
+        jz[zh] = decoded_total(jr, jru, 2 * K)
         wait_for(rsem, JZ, jz, NZ - 1)
         share = total_of(jz, NZ)
         for o in range(2):
@@ -309,6 +349,8 @@
     wait_for(ssem, VEC, vrecv, n_row - 1)
     wait_for(ssem, HY, hr, NY - 1)
     wait_for(ssem, JY, jr, NY - 1)
+    wait_for(ssem, HU, hru, NY - 1)
+    wait_for(ssem, JU, jru, NY - 1)
 
 
 def solution(mesh):
@@ -336,10 +378,14 @@
                 pltpu.VMEM((jq, T, T), BF16),
                 pltpu.SMEM((1, 1, hq), jnp.int32),
                 pltpu.SMEM((1, 1, jq), jnp.int32),
-                pltpu.VMEM((NY, K, T), F32),
-                pltpu.VMEM((NY, K, T), F32),
-                pltpu.VMEM((NY, 2 * K, T), F32),
-                pltpu.VMEM((NY, 2 * K, T), F32),
+                pltpu.VMEM((NY, K, T), jnp.int16),
+                pltpu.VMEM((NY, K, T), jnp.int16),
+                pltpu.VMEM((NY, 2 * K, T), jnp.int16),
+                pltpu.VMEM((NY, 2 * K, T), jnp.int16),
+                pltpu.VMEM((NY, 1, T), F32),
+                pltpu.VMEM((NY, 1, T), F32),
+                pltpu.VMEM((NY, 1, T), F32),
+                pltpu.VMEM((NY, 1, T), F32),
                 pltpu.VMEM((NZ, K, T), F32),
                 pltpu.VMEM((NZ, 2 * K, T), F32),
                 pltpu.VMEM((1, K, T), F32),
@@ -350,8 +396,8 @@
                 pltpu.VMEM((NX * NY, 4, T), F32),
                 pltpu.VMEM((n_row // NX, 4, T), F32),
                 pltpu.SemaphoreType.DMA((5,)),
-                pltpu.SemaphoreType.DMA((10,)),
-                pltpu.SemaphoreType.DMA((10,)),
+                pltpu.SemaphoreType.DMA((12,)),
+                pltpu.SemaphoreType.DMA((12,)),
             ],
             compiler_params=pltpu.CompilerParams(
                 collective_id=0, has_side_effects=True, vmem_limit_bytes=60 * 1024 * 1024

time: 52.8 us -> 51.8 us (0.981)
  Pallas kernels: 50 us -> 49.1 us
    pallas_call x1, Pallas kernels: 50 us -> 49.1 us  [per_device(): pl.pallas_call(functools.partial(kernel, n_row, n_col, float(total_rows))...]
where the time goes in v3:
time: 51.8 us; the launch traced here: 51.6 us
  Pallas kernels  49.1 us (95%)
  local copies, waits for them, and re-layouts  1.91 us (4%)
  between operations  0.65 us (1%)
    pallas_call x1, Pallas kernels, per_device(): pl.pallas_call(functools.partial(kernel, n_row, n_col, float(total_rows))...  49.1 us
    unnamed x4, local copies, waits for them, and re-layouts  1.91 us

profile of v3, /device:TPU:1, one launch (start us, length us, event | category | flops | bytes accessed | tf_op | source)
XLA Modules:
  0.0 51.6 jit_solution(15050903566370613801)
XLA Ops:
  0.6 49.1 %shard_map.68 = (f32[1,16,32]{2,1,0:T(8,128)}, f32[1,2,16,16]{3,2,1,0:T(8,128)}) custom-call(bf16[1,16,32]{2,1,0:T(8,128)(2,1)} %vec_hbm.1, bf16[32,128,128]{2,1,0:T(8,128)(2,1)} %bitcast.2, s32[1,1,32]{2,1,0:T(1,128)} %hl_hbm.1, bf16[12,128,128]{2,1,0:T(8,128)(2,1)} %bitcast.3, s32[1,1,12]{2,1,0:T(1,128)} %jl_hbm.1), custom_call_target="tpu_custom_call" | custom-call | tf_op jit(solution)/shard_map/pallas_call | solution.py:364
  49.7 0.0 copy-start
  49.7 1.3 %copy.9 = f32[1,16,32]{2,1,0:T(8,128)} copy(f32[1,16,32]{2,1,0:T(8,128)} %get-tuple-element.4) | data formatting | bytes 4096
  51.0 0.0 copy-done
  51.0 0.6 %copy.10 = f32[1,2,16,16]{3,2,1,0:T(8,128)} copy(f32[1,2,16,16]{3,2,1,0:T(8,128)S(1)} %copy-done) | data formatting | bytes 4096
Async XLA Ops:
  49.7 1.3 %copy-start = (f32[1,2,16,16]{3,2,1,0:T(8,128)S(1)}, f32[1,2,16,16]{3,2,1,0:T(8,128)}, u32[]{:S(2)}) copy-start(f32[1,2,16,16]{3,2,1,0:T(8,128)} %get-tuple-element.5) | copy-start | bytes 6148

commit v4 on v3

--- a/solution.py
+++ b/solution.py
@@ -323,15 +323,28 @@
         )
     basis_ref[0] = own_lanes[:, :32]
 
+    scaled = root / jnp.sqrt(scale)
+
     @pl.when(jnp.logical_not(at_last))
     def _():
         wait_for(rsem, CB, cb, n_in)
+
+    @pl.when(at_last)
+    def _():
+        wait_for(rsem, CB, cb, n_in - 1)
+
+    part = total_of(cb, n_in)
+    for o in range(2):
+        cross = from_flat([part[2 * o : 2 * o + 1], part[2 * o + 1 : 2 * o + 2]])
+        elem_ref[0, o] = small_dot(scaled, cross, group)[:, :K]
+
+    @pl.when(jnp.logical_not(at_last))
+    def _():
         wait_for(ssem, HZ, hz, 1)
         wait_for(ssem, JZ, jz, 1)
 
     @pl.when(at_last)
     def _():
-        wait_for(rsem, CB, cb, n_in - 1)
         wait_for(ssem, GA, ga, NX * NY - 1)
         for _ in range(NZ - 1):
             wait_for(ssem, PZ, pz, 1)
@@ -341,11 +354,6 @@
                 wait_for(ssem, at, buf, n_in)
             wait_for(ssem, at, buf, n_in - 1)
 
-    part = total_of(cb, n_in)
-    for o in range(2):
-        cross = from_flat([part[2 * o : 2 * o + 1], part[2 * o + 1 : 2 * o + 2]])
-        elements = small_dot(root, cross, group) / jnp.sqrt(scale)
-        elem_ref[0, o] = elements[:, :K]
     wait_for(ssem, VEC, vrecv, n_row - 1)
     wait_for(ssem, HY, hr, NY - 1)
     wait_for(ssem, JY, jr, NY - 1)
@@ -364,8 +372,8 @@
         return pl.pallas_call(
             functools.partial(kernel, n_row, n_col, float(total_rows)),
             out_shape=(
-                jax.ShapeDtypeStruct((1, K, 32), F32),
-                jax.ShapeDtypeStruct((1, 2, K, K), F32),
+                pltpu.VMEM((1, K, 32), F32),
+                pltpu.VMEM((1, 2, K, K), F32),
             ),
             in_specs=[hbm] * 5,
             out_specs=(vmem, vmem),

time: 51.8 us -> 50.5 us (0.975)
  local copies, waits for them, and re-layouts: 1.91 us -> 1.21 us
  Pallas kernels: 49.1 us -> 48.5 us
    unnamed x4 -> x2, local copies, waits for them, and re-layouts: 1.91 us -> 1.21 us
    pallas_call x1, Pallas kernels: 49.1 us -> 48.5 us  [per_device(): pl.pallas_call(functools.partial(kernel, n_row, n_col, float(total_rows))...]
where the time goes in v4:
time: 50.5 us; the launch traced here: 50.3 us
  Pallas kernels  48.5 us (96%)
  local copies, waits for them, and re-layouts  1.21 us (2%)
  between operations  0.64 us (1%)
    pallas_call x1, Pallas kernels, per_device(): pl.pallas_call(functools.partial(kernel, n_row, n_col, float(total_rows))...  48.5 us
    unnamed x2, local copies, waits for them, and re-layouts  1.21 us

profile of v4, /device:TPU:1, one launch (start us, length us, event | category | flops | bytes accessed | tf_op | source)
XLA Modules:
  0.0 50.3 jit_solution(17107847260618771981)
XLA Ops:
  0.6 48.5 %shard_map.68 = (f32[1,16,32]{2,1,0:T(8,128)S(1)}, f32[1,2,16,16]{3,2,1,0:T(8,128)S(1)}) custom-call(bf16[1,16,32]{2,1,0:T(8,128)(2,1)} %vec_hbm.1, bf16[32,128,128]{2,1,0:T(8,128)(2,1)} %bitcast.2, s32[1,1,32]{2,1,0:T(1,128)} %hl_hbm.1, bf16[12,128,128]{2,1,0:T(8,128)(2,1)} %bitcast.3, s32[1,1,12]{2,1,0:T(1,128)} %jl_hbm.1), custom_call_target="tpu_custom_call" | custom-call | tf_op jit(solution)/shard_map/pallas_call | solution.py:372
  49.1 0.6 %copy.9 = f32[1,16,32]{2,1,0:T(8,128)} copy(f32[1,16,32]{2,1,0:T(8,128)S(1)} %get-tuple-element.2) | data formatting | bytes 4096
  49.7 0.6 %copy.10 = f32[1,2,16,16]{3,2,1,0:T(8,128)} copy(f32[1,2,16,16]{3,2,1,0:T(8,128)S(1)} %get-tuple-element.3) | data formatting | bytes 4096

commit v5 on v4

--- a/solution.py
+++ b/solution.py
@@ -14,7 +14,7 @@
 NY = 8
 NZ = 4
 NX = 4
-VEC, HY, JY, HZ, JZ, PZ, GA, CA, GB, CB, HU, JU = range(12)
+VEC, HY, JY, JZ, PZ, GA, CA, GB, CB, HU, JU = range(11)
 K = 16
 T = 128
 NT = (((1,), (1,)), ((), ()))
@@ -61,18 +61,22 @@
     return steps, units
 
 
-def decoded_total(steps, units, rows):
+def spread_units(units, rows, count):
     own = iota((rows, T), 1) == iota((rows, T), 0)
-    spread = jnp.concatenate(
+    placed = jnp.concatenate(
         [
             jnp.where(own, jnp.broadcast_to(units[d], (rows, T)), 0.0).astype(BF16)
-            for d in range(NY)
+            for d in range(count)
         ],
         axis=0,
     )
-    unit = jnp.dot(spread, jnp.ones((T, T), BF16), preferred_element_type=F32)
+    return jnp.dot(placed, jnp.ones((T, T), BF16), preferred_element_type=F32)
+
+
+def decoded_total(steps, unit, rows, count):
     parts = [
-        steps[d].astype(jnp.int32).astype(F32) * unit[d * rows : (d + 1) * rows] for d in range(NY)
+        steps[d].astype(jnp.int32).astype(F32) * unit[d * rows : (d + 1) * rows]
+        for d in range(count)
     ]
     while len(parts) > 1:
         parts = [parts[k] + parts[k + 1] for k in range(0, len(parts), 2)]
@@ -100,8 +104,8 @@
 def kernel(
     n_row, n_col, total_rows,
     vec_hbm, ht_hbm, hl_hbm, jt_hbm, jl_hbm, basis_ref, elem_ref,
-    vloc, vsend, vrecv, vblk, ht, jt, hl, jl, hs, hr, js, jr, hsu, hru, jsu, jru, hz, jz, pz, gs, ga, gb, cs, ca, cb,
-    lsem, ssem, rsem,
+    vloc, vsend, vrecv, vblk, ht, jt, hl, jl, hs, hr, js, jr, hsu, hru, jsu, jru, jz, pz, gs, ga, gb, cs, ca, cb,
+    lsem, ssem, rsem, ready,
 ):
     me_r = lax.axis_index("row")
     me_c = lax.axis_index("col")
@@ -136,7 +140,7 @@
         return {"row": x * n_in + to % n_in, "col": (to // n_in) * NY + y}
 
     def at_collector(d):
-        return {"col": last * NY + y}
+        return {"col": last * NY + wrap(y + d, NY)}
 
     codes = [
         pltpu.make_async_copy(hl_hbm, hl, lsem.at[3]),
@@ -187,6 +191,11 @@
         load.wait()
 
     pl.semaphore_wait(barrier, n_row - 1 + NY - 1 + NZ - 1)
+    @pl.when(at_last)
+    def _():
+        for d in range(1, NZ):
+            pl.semaphore_signal(ready, inc=1, device_id=at_z(d), device_id_type=MESH)
+
     send_all(VEC, at_row, n_row - 1, lambda d: vsend, vrecv.at[me_r])
     loads[1].wait()
     loads[2].wait()
@@ -226,15 +235,6 @@
                 piece = pltpu.roll(piece, shift, 1)
             out = piece if out is None else jnp.where(lane32 == z, piece, out)
         return out
-
-    h_total = products(hl, ht, ht.shape[0], 8)
-    for yh in range(2):
-        for s in range(4):
-            hs[yh * 4 + s], hsu[yh * 4 + s] = coded(packed(h_total, 0, yh, s), 0)
-    hr[y] = hs[y]
-    hru[y] = hsu[y]
-    send_all(HU, at_y, NY - 1, lambda d: hsu.at[wrap(y + d, NY)], hru.at[y])
-    send_all(HY, at_y, NY - 1, lambda d: hs.at[wrap(y + d, NY)], hr.at[y])
 
     j_total = products(jl, jt, jt.shape[0], 16)
     for yh in range(2):
@@ -248,25 +248,43 @@
     jru[y] = jsu[y]
     send_all(JU, at_y, NY - 1, lambda d: jsu.at[wrap(y + d, NY)], jru.at[y])
     send_all(JY, at_y, NY - 1, lambda d: js.at[wrap(y + d, NY)], jr.at[y])
-
-    wait_for(rsem, HU, hru, NY - 1)
-    wait_for(rsem, HY, hr, NY - 1)
-    hz[zh] = decoded_total(hr, hru, K)
+    h_total = products(hl, ht, ht.shape[0], 8)
+    for yh in range(2):
+        for s in range(4):
+            hs[yh * 4 + s], hsu[yh * 4 + s] = coded(packed(h_total, 0, yh, s), 0)
+
+    def decode_j():
+        wait_for(rsem, JU, jru, NY - 1)
+        unit = spread_units(jru, 2 * K, NY)
+        wait_for(rsem, JY, jr, NY - 1)
+        jz[zh] = decoded_total(jr, unit, 2 * K, NY)
 
     @pl.when(jnp.logical_not(at_last))
     def _():
-        send_all(HZ, at_collector, 1, lambda d: hz.at[zh], hz.at[zh])
-        wait_for(rsem, JU, jru, NY - 1)
-        wait_for(rsem, JY, jr, NY - 1)
-        jz[zh] = decoded_total(jr, jru, 2 * K)
-        send_all(JZ, at_collector, 1, lambda d: jz.at[zh], jz.at[zh])
+        pl.semaphore_wait(ready, 1)
+        send_all(
+            HU, lambda d: at_collector(d - 1), NY, lambda d: hsu.at[wrap(y + d - 1, NY)], hru.at[me_c]
+        )
+        send_all(
+            HY, lambda d: at_collector(d - 1), NY, lambda d: hs.at[wrap(y + d - 1, NY)], hr.at[me_c]
+        )
+        decode_j()
+        send_all(JZ, lambda d: at_collector(0), 1, lambda d: jz.at[zh], jz.at[zh])
         wait_for(rsem, PZ, pz, 1)
+        wait_for(rsem, GB, gb, n_in)
 
     @pl.when(at_last)
     def _():
         slot = y * NX + x
-        wait_for(rsem, HZ, hz, NZ - 1)
-        proj = total_of(hz, NZ)
+        hr[me_c] = hs[y]
+        hru[me_c] = hsu[y]
+        send_all(HU, at_collector, NY - 1, lambda d: hsu.at[wrap(y + d, NY)], hru.at[me_c])
+        send_all(HY, at_collector, NY - 1, lambda d: hs.at[wrap(y + d, NY)], hr.at[me_c])
+        decode_j()
+        wait_for(rsem, HU, hru, n_col - 1)
+        unit = spread_units(hru, K, n_col)
+        wait_for(rsem, HY, hr, n_col - 1)
+        proj = decoded_total(hr, unit, K, n_col)
         pz[0] = proj
         rows = flat_rows(long_dot(proj, jnp.concatenate([proj] * 8, axis=0)))
         for h in range(2):
@@ -275,9 +293,6 @@
         send_all(GA, at_plane, NX * NY - 1, lambda d: gs, ga.at[slot])
         send_all(PZ, at_z, NZ - 1, lambda d: pz.at[0], pz.at[0])
 
-        wait_for(rsem, JU, jru, NY - 1)
-        wait_for(rsem, JY, jr, NY - 1)
-        jz[zh] = decoded_total(jr, jru, 2 * K)
         wait_for(rsem, JZ, jz, NZ - 1)
         share = total_of(jz, NZ)
         for o in range(2):
@@ -296,10 +311,6 @@
         cb[inner] = total_of(ca, NX * NY)
         send_all(CB, at_line, NZ * n_in - 1, lambda d: cb.at[inner], cb.at[inner])
         wait_for(rsem, GB, gb, n_in - 1)
-
-    @pl.when(jnp.logical_not(at_last))
-    def _():
-        wait_for(rsem, GB, gb, n_in)
 
     part = total_of(gb, n_in)
     square = jnp.sum(jnp.sum(part * part, axis=1, keepdims=True), axis=0, keepdims=True)
@@ -340,11 +351,14 @@
 
     @pl.when(jnp.logical_not(at_last))
     def _():
-        wait_for(ssem, HZ, hz, 1)
+        wait_for(ssem, HU, hru, NY)
+        wait_for(ssem, HY, hr, NY)
         wait_for(ssem, JZ, jz, 1)
 
     @pl.when(at_last)
     def _():
+        wait_for(ssem, HU, hru, NY - 1)
+        wait_for(ssem, HY, hr, NY - 1)
         wait_for(ssem, GA, ga, NX * NY - 1)
         for _ in range(NZ - 1):
             wait_for(ssem, PZ, pz, 1)
@@ -355,10 +369,8 @@
             wait_for(ssem, at, buf, n_in - 1)
 
     wait_for(ssem, VEC, vrecv, n_row - 1)
-    wait_for(ssem, HY, hr, NY - 1)
+    wait_for(ssem, JU, jru, NY - 1)
     wait_for(ssem, JY, jr, NY - 1)
-    wait_for(ssem, HU, hru, NY - 1)
-    wait_for(ssem, JU, jru, NY - 1)
 
 
 def solution(mesh):
@@ -387,14 +399,13 @@
                 pltpu.SMEM((1, 1, hq), jnp.int32),
                 pltpu.SMEM((1, 1, jq), jnp.int32),
                 pltpu.VMEM((NY, K, T), jnp.int16),
-                pltpu.VMEM((NY, K, T), jnp.int16),
+                pltpu.VMEM((n_col, K, T), jnp.int16),
                 pltpu.VMEM((NY, 2 * K, T), jnp.int16),
                 pltpu.VMEM((NY, 2 * K, T), jnp.int16),
                 pltpu.VMEM((NY, 1, T), F32),
+                pltpu.VMEM((n_col, 1, T), F32),
                 pltpu.VMEM((NY, 1, T), F32),
                 pltpu.VMEM((NY, 1, T), F32),
-                pltpu.VMEM((NY, 1, T), F32),
-                pltpu.VMEM((NZ, K, T), F32),
                 pltpu.VMEM((NZ, 2 * K, T), F32),
                 pltpu.VMEM((1, K, T), F32),
                 pltpu.VMEM((2, T), F32),
@@ -406,6 +417,7 @@
                 pltpu.SemaphoreType.DMA((5,)),
                 pltpu.SemaphoreType.DMA((12,)),
                 pltpu.SemaphoreType.DMA((12,)),
+                pltpu.SemaphoreType.REGULAR,
             ],
             compiler_params=pltpu.CompilerParams(
                 collective_id=0, has_side_effects=True, vmem_limit_bytes=60 * 1024 * 1024

time: 50.5 us -> 49.3 us (0.976)
  Pallas kernels: 48.5 us -> 47.3 us
    pallas_call x1, Pallas kernels: 48.5 us -> 47.3 us  [per_device(): pl.pallas_call(functools.partial(kernel, n_row, n_col, float(total_rows))...]
where the time goes in v5:
time: 49.3 us; the launch traced here: 49.1 us
  Pallas kernels  47.3 us (96%)
  local copies, waits for them, and re-layouts  1.21 us (2%)
  between operations  0.64 us (1%)
    pallas_call x1, Pallas kernels, per_device(): pl.pallas_call(functools.partial(kernel, n_row, n_col, float(total_rows))...  47.3 us
    unnamed x2, local copies, waits for them, and re-layouts  1.21 us

profile of v5, /device:TPU:1, one launch (start us, length us, event | category | flops | bytes accessed | tf_op | source)
XLA Modules:
  0.0 49.1 jit_solution(1632112128908766881)
XLA Ops:
  0.6 47.3 %shard_map.68 = (f32[1,16,32]{2,1,0:T(8,128)S(1)}, f32[1,2,16,16]{3,2,1,0:T(8,128)S(1)}) custom-call(bf16[1,16,32]{2,1,0:T(8,128)(2,1)} %vec_hbm.1, bf16[32,128,128]{2,1,0:T(8,128)(2,1)} %bitcast.2, s32[1,1,32]{2,1,0:T(1,128)} %hl_hbm.1, bf16[12,128,128]{2,1,0:T(8,128)(2,1)} %bitcast.3, s32[1,1,12]{2,1,0:T(1,128)} %jl_hbm.1), custom_call_target="tpu_custom_call" | custom-call | tf_op jit(solution)/shard_map/pallas_call | solution.py:384
  47.9 0.6 %copy.9 = f32[1,16,32]{2,1,0:T(8,128)} copy(f32[1,16,32]{2,1,0:T(8,128)S(1)} %get-tuple-element.2) | data formatting | bytes 4096
  48.5 0.6 %copy.10 = f32[1,2,16,16]{3,2,1,0:T(8,128)} copy(f32[1,2,16,16]{3,2,1,0:T(8,128)S(1)} %get-tuple-element.3) | data formatting | bytes 4096

commit v6 on v5

--- a/solution.py
+++ b/solution.py
@@ -14,6 +14,7 @@
 NY = 8
 NZ = 4
 NX = 4
+FAR_FIRST = (4, 3, 5, 2, 6, 1, 7)
 VEC, HY, JY, JZ, PZ, GA, CA, GB, CB, HU, JU = range(11)
 K = 16
 T = 128
@@ -158,14 +159,18 @@
             return carry
         return step
 
-    def send_all(at, where, count, src, dst):
+    def send_all(at, where, count, src, dst, order=None):
         def step(d, carry):
             pltpu.make_async_remote_copy(
                 src_ref=src(d), dst_ref=dst, send_sem=ssem.at[at], recv_sem=rsem.at[at],
                 device_id=where(d), device_id_type=MESH,
             ).start()
             return carry
-        lax.fori_loop(1, count + 1, step, 0)
+        if order is None:
+            lax.fori_loop(1, count + 1, step, 0)
+        else:
+            for d in order:
+                step(d, 0)
 
     def wait_for(sem, at, buf, count):
         part = buf.at[pl.ds(0, count)]
@@ -246,8 +251,8 @@
             jsu[yh * 4 + s] = first_units + second_units
     jr[y] = js[y]
     jru[y] = jsu[y]
-    send_all(JU, at_y, NY - 1, lambda d: jsu.at[wrap(y + d, NY)], jru.at[y])
-    send_all(JY, at_y, NY - 1, lambda d: js.at[wrap(y + d, NY)], jr.at[y])
+    send_all(JU, at_y, NY - 1, lambda d: jsu.at[wrap(y + d, NY)], jru.at[y], FAR_FIRST)
+    send_all(JY, at_y, NY - 1, lambda d: js.at[wrap(y + d, NY)], jr.at[y], FAR_FIRST)
     h_total = products(hl, ht, ht.shape[0], 8)
     for yh in range(2):
         for s in range(4):
@@ -263,10 +268,10 @@
     def _():
         pl.semaphore_wait(ready, 1)
         send_all(
-            HU, lambda d: at_collector(d - 1), NY, lambda d: hsu.at[wrap(y + d - 1, NY)], hru.at[me_c]
+            HU, at_collector, NY, lambda d: hsu.at[wrap(y + d, NY)], hru.at[me_c], FAR_FIRST + (0,)
         )
         send_all(
-            HY, lambda d: at_collector(d - 1), NY, lambda d: hs.at[wrap(y + d - 1, NY)], hr.at[me_c]
+            HY, at_collector, NY, lambda d: hs.at[wrap(y + d, NY)], hr.at[me_c], FAR_FIRST + (0,)
         )
         decode_j()
         send_all(JZ, lambda d: at_collector(0), 1, lambda d: jz.at[zh], jz.at[zh])
@@ -278,8 +283,12 @@
         slot = y * NX + x
         hr[me_c] = hs[y]
         hru[me_c] = hsu[y]
-        send_all(HU, at_collector, NY - 1, lambda d: hsu.at[wrap(y + d, NY)], hru.at[me_c])
-        send_all(HY, at_collector, NY - 1, lambda d: hs.at[wrap(y + d, NY)], hr.at[me_c])
+        send_all(
+            HU, at_collector, NY - 1, lambda d: hsu.at[wrap(y + d, NY)], hru.at[me_c], FAR_FIRST
+        )
+        send_all(
+            HY, at_collector, NY - 1, lambda d: hs.at[wrap(y + d, NY)], hr.at[me_c], FAR_FIRST
+        )
         decode_j()
         wait_for(rsem, HU, hru, n_col - 1)
         unit = spread_units(hru, K, n_col)

time: 49.3 us -> 49 us (level)
  no operation moved by 1% of the time
where the time goes in v6:
time: 49 us; the launch traced here: 48.8 us
  Pallas kernels  47 us (96%)
  local copies, waits for them, and re-layouts  1.21 us (2%)
  between operations  0.64 us (1%)
    pallas_call x1, Pallas kernels, per_device(): pl.pallas_call(functools.partial(kernel, n_row, n_col, float(total_rows))...  47 us
    unnamed x2, local copies, waits for them, and re-layouts  1.21 us

profile of v6, /device:TPU:1, one launch (start us, length us, event | category | flops | bytes accessed | tf_op | source)
XLA Modules:
  0.0 48.8 jit_solution(17148866682517769147)
XLA Ops:
  0.6 47.0 %shard_map.68 = (f32[1,16,32]{2,1,0:T(8,128)S(1)}, f32[1,2,16,16]{3,2,1,0:T(8,128)S(1)}) custom-call(bf16[1,16,32]{2,1,0:T(8,128)(2,1)} %vec_hbm.1, bf16[32,128,128]{2,1,0:T(8,128)(2,1)} %bitcast.2, s32[1,1,32]{2,1,0:T(1,128)} %hl_hbm.1, bf16[12,128,128]{2,1,0:T(8,128)(2,1)} %bitcast.3, s32[1,1,12]{2,1,0:T(1,128)} %jl_hbm.1), custom_call_target="tpu_custom_call" | custom-call | tf_op jit(solution)/shard_map/pallas_call | solution.py:393
  47.6 0.6 %copy.9 = f32[1,16,32]{2,1,0:T(8,128)} copy(f32[1,16,32]{2,1,0:T(8,128)S(1)} %get-tuple-element.2) | data formatting | bytes 4096
  48.2 0.6 %copy.10 = f32[1,2,16,16]{3,2,1,0:T(8,128)} copy(f32[1,2,16,16]{3,2,1,0:T(8,128)S(1)} %get-tuple-element.3) | data formatting | bytes 4096

commit v7 on v6

--- a/solution.py
+++ b/solution.py
@@ -132,7 +132,7 @@
         return {"col": wrap(zh + d, NZ) * NY + y}
 
     def at_plane(d):
-        to = y * NX + x + d
+        to = y * NX + x + 1 + wrap(d + 12, NX * NY - 1)
         to = wrap(to, NX * NY)
         return {"row": (to % NX) * n_in + inner, "col": zh * NY + to // NX}
 

time: 49 us -> 48.9 us (level)
  no operation moved by 1% of the time
where the time goes in v7:
time: 48.9 us; the launch traced here: 48.7 us
  Pallas kernels  46.9 us (96%)
  local copies, waits for them, and re-layouts  1.21 us (2%)
  between operations  0.64 us (1%)
    pallas_call x1, Pallas kernels, per_device(): pl.pallas_call(functools.partial(kernel, n_row, n_col, float(total_rows))...  46.9 us
    unnamed x2, local copies, waits for them, and re-layouts  1.21 us

profile of v7, /device:TPU:1, one launch (start us, length us, event | category | flops | bytes accessed | tf_op | source)
XLA Modules:
  0.0 48.7 jit_solution(14487057621797276792)
XLA Ops:
  0.6 46.9 %shard_map.68 = (f32[1,16,32]{2,1,0:T(8,128)S(1)}, f32[1,2,16,16]{3,2,1,0:T(8,128)S(1)}) custom-call(bf16[1,16,32]{2,1,0:T(8,128)(2,1)} %vec_hbm.1, bf16[32,128,128]{2,1,0:T(8,128)(2,1)} %bitcast.2, s32[1,1,32]{2,1,0:T(1,128)} %hl_hbm.1, bf16[12,128,128]{2,1,0:T(8,128)(2,1)} %bitcast.3, s32[1,1,12]{2,1,0:T(1,128)} %jl_hbm.1), custom_call_target="tpu_custom_call" | custom-call | tf_op jit(solution)/shard_map/pallas_call | solution.py:393
  47.5 0.6 %copy.9 = f32[1,16,32]{2,1,0:T(8,128)} copy(f32[1,16,32]{2,1,0:T(8,128)S(1)} %get-tuple-element.2) | data formatting | bytes 4096
  48.1 0.6 %copy.10 = f32[1,2,16,16]{3,2,1,0:T(8,128)} copy(f32[1,2,16,16]{3,2,1,0:T(8,128)S(1)} %get-tuple-element.3) | data formatting | bytes 4096
